TPU v7x, 512 devices: a whole 4x4x16 slice. The times are simulated.
512 devices in a mesh: frames: 64 (over z, y_hi, core), mp: 4 (over x), dp: 2 (over y_lo).
Axes of the slice: x: 4, y: 4 (y_hi: 2, y_lo: 2; y = y_hi * 2 + y_lo), z: 16, core: 2. Of those that a mesh axis runs over, the one named last changes fastest.
Arguments:
- projections: bfloat16 [2, 128, 96, 3, 3584], P('dp', 'frames', None, None, 'mp'), may hold values from -18 to 18
- perturbation: bfloat16 [2, 128, 96, 3, 3584], P('dp', 'frames', None, None, 'mp'), may hold values from -44 to 44
- out_weight: bfloat16 [3584, 3584], P('frames', 'mp'), may hold values from -0.09375 to 0.09375
- norm_gain: float32 [3584], P('mp'), may hold values from 0.25 to 1.75
- live_counts: int32 [2, 128], P('dp'), may hold values from 72 to 96, as said below
Outputs:
- features: bfloat16 [2, 128, 96, 3584], P('dp', 'frames', None, 'mp')
- penalty: float32 [2], P('dp')
- gain_grad: float32 [3584], P('mp')
Inputs may be any that keep to these rules, and one draw needn't show every extreme that they name: `live_counts`: in each clip one slot has all 96 tokens live and another has 72 live.
All inputs are finite; a program needn't handle non-finite values.
Results may differ from a plain program's by a relative error of at most 0.0057.
Values may be sent and summed in bfloat16 or wider, within the bound.
A program may use at most 64 MiB of HBM per device.

v0:
```python
import math
import jax
import jax.numpy as jnp
from jax import lax
from jax.sharding import PartitionSpec as P

HEAD_DIM = 128
sigma_noise = 0.25
epsilon = 1e-06


def padded(cells, sides, width):
    for axis, dim in sides:
        count = lax.axis_size(axis)
        ends = count - 1
        head = lax.slice_in_dim(cells, 0, width, axis=dim)
        tail = lax.slice_in_dim(cells, cells.shape[dim] - width, cells.shape[dim], axis=dim)
        cells = jnp.concatenate(
            [
                lax.ppermute(tail, axis, [(i, (i + 1) % count) for i in range(ends)]),
                cells,
                lax.ppermute(head, axis, [((i + 1) % count, i) for i in range(ends)]),
            ],
            axis=dim,
        )
    return cells


def split_heads(tensor):
    return tensor.reshape(tensor.shape[:-1] + (tensor.shape[-1] // HEAD_DIM, HEAD_DIM))


def attend(query_rows, key_rows, value_rows, key_live):
    scores = jnp.einsum(
        "wrhe,wmhe->whrm",
        split_heads(query_rows),
        split_heads(key_rows),
        preferred_element_type=jnp.float32,
    ) * (1.0 / math.sqrt(HEAD_DIM))
    live_float = key_live[:, None, None, :]
    masked = jnp.where(live_float, scores, -1e30)
    largest = jnp.max(masked, axis=-1, keepdims=True)
    weights = jnp.exp(masked - largest) * live_float.astype(jnp.float32)
    probabilities = (weights / jnp.sum(weights, axis=-1, keepdims=True)).astype(jnp.bfloat16)
    mixed = jnp.einsum(
        "whrm,wmhe->wrhe",
        probabilities,
        split_heads(value_rows),
        preferred_element_type=jnp.float32,
    )
    return mixed.astype(jnp.bfloat16).reshape(query_rows.shape)


def attend_each(query_rows, key_rows, value_rows, key_live):

    def one_window(item):
        return attend(item[0][None], item[1][None], item[2][None], item[3][None])[0]

    return lax.map(one_window, (query_rows, key_rows, value_rows, key_live))


def local(projections, perturbation, out_weight, norm_gain, live_counts):
    tile_len = projections.shape[2]
    local_width = projections.shape[4]
    slab_count = lax.axis_size("frames")
    slab_index = lax.axis_index("frames")
    model_width = local_width * lax.axis_size("mp")
    token_total = projections.shape[1] * slab_count * tile_len
    perturbed = (
        projections.astype(jnp.float32) + sigma_noise * perturbation.astype(jnp.float32)
    ).astype(jnp.bfloat16)
    streams = jnp.concatenate([projections, perturbed], axis=0)
    padded_counts = jnp.pad(live_counts[0], (1, 1))
    nearby = lax.dynamic_slice_in_dim(padded_counts, 2 * slab_index, 4)
    token_pos = jnp.arange(tile_len)
    live_near = token_pos[None, :] < nearby[:, None]
    key_values = streams[:, :, :, 1:, :]
    widened = padded(key_values, (("frames", 1),), 1)
    grouped = widened.reshape(4, 2 * tile_len, 2, local_width)
    query_rows = streams[:, :, :, 0, :].reshape(4, tile_len, local_width)
    key_live = jnp.tile(live_near.reshape(2, 2 * tile_len), (2, 1))
    attended = attend_each(query_rows, grouped[:, :, 0], grouped[:, :, 1], key_live)
    attended = attended.reshape(2, 2, tile_len, local_width)
    gathered = lax.all_gather(attended, "mp", axis=3, tiled=True)
    flat_rows = gathered.reshape(-1, model_width)
    projected = jnp.dot(
        flat_rows,
        lax.all_gather(out_weight, "frames", axis=0, tiled=True),
        preferred_element_type=jnp.float32,
    )
    projected = projected.reshape(2, 2, tile_len, local_width)
    squares = lax.psum(jnp.sum(projected * projected, axis=-1), "mp")
    normed = projected * lax.rsqrt(squares / model_width + epsilon)[..., None]
    own_live = live_near[1:3].astype(jnp.float32)[:, :, None]
    features = (normed[0] * norm_gain * own_live).astype(jnp.bfloat16)[None]
    difference = (normed[1] - normed[0]) * own_live
    feature_sums = jnp.sum(difference * difference, axis=(0, 1))
    local_penalty = jnp.sum(feature_sums * norm_gain * norm_gain).reshape(1)
    penalty = lax.psum(local_penalty, ("frames", "mp")) / (
        sigma_noise * sigma_noise * token_total * model_width
    )
    gain_grad = (
        norm_gain
        * lax.psum(feature_sums, ("frames", "dp"))
        / (sigma_noise * sigma_noise * token_total)
    )
    return (features, penalty, gain_grad)


def solution(mesh):
    placed = (
        P("dp", "frames", None, None, "mp"),
        P("dp", "frames", None, None, "mp"),
        P("frames", "mp"),
        P("mp"),
        P("dp", None),
    )
    return jax.shard_map(
        local,
        mesh=mesh,
        in_specs=placed,
        out_specs=(P("dp", "frames", None, "mp"), P("dp"), P("mp")),
        check_vma=False,
    )
```

profile of v0, /device:TPU:2, one launch (start us, length us, event | category | flops | bytes accessed | tf_op | source)
XLA Modules:
  0.0 1192.0 jit_solution(10483000948008665854)
XLA Ops:
  7.2 1.9 add_convert_fusion
  9.2 1.2 fusion.25
  10.4 2.6 collective-permute-start
  13.0 1.3 collective-permute-start.1
  15.0 4.5 collective-permute-done.1
  19.5 1.7 pad_maximum_fusion
  21.5 1.3 slice_bitcast_fusion
  22.8 22.9 %while.10 = (s32[]{:T(128)}, bf16[4,96,896]{2,1,0:T(8,128)(2,1)}, bf16[4,192,896]{2,1,0:T(8,128)(2,1)}, pred[4,192]{1,0:T(4,128)(4,1)S(1)}, bf16[4,96,896]{2,1,0...) while((s32[]{:T(128)}, bf16[4,96,896]{2,1,0:T(8,128)(2,1)}, bf16[4,192,896]{2,1,0:T(8,128)(2,1)}, ...), condition=%wide.region_3.4_spmd, body=%wide.region_0.3_spmd.sunk | while | flops 67049856 | bytes 5857369 | solution.py:59
  22.8 1.0 constant_dynamic-slice_fusion.5
  24.5 1.5 fusion.45
  26.4 1.4 fusion.46
  27.8 0.7 bitcast_dynamic-update-slice_fusion.2
  28.5 1.0 constant_dynamic-slice_fusion.5
  30.2 1.5 fusion.45
  32.1 1.4 fusion.46
  34.2 1.0 constant_dynamic-slice_fusion.5
  36.0 1.5 fusion.45
  37.9 1.4 fusion.46
  39.3 0.7 bitcast_dynamic-update-slice_fusion.2
  40.0 1.0 constant_dynamic-slice_fusion.5
  41.7 1.5 fusion.45
  43.6 1.4 fusion.46
  45.0 0.7 bitcast_dynamic-update-slice_fusion.2
  45.8 0.7 all-gather.5.cloned.1.call-update
  46.5 59.2 %all-gather.3.cloned.1.call-done = bf16[2,2,96,3584]{3,2,1,0:T(8,128)(2,1)} async-done(((bf16[2,2,96,896]{3,2,1,0:T(8,128)(2,1)}), bf16[2,2,96,3584]{3,2,1,0:T(8,128)(2,1)}) %all-gather.3.cloned.1.call-update) | async-done | bytes 2752528 | tf_op jit(solution)/shard_map/all_gather | solution.py:84
  105.8 162.8 %all-gather.5.cloned.1.call-done = bf16[3584,896]{1,0:T(8,128)(2,1)} async-done(((bf16[56,896]{1,0:T(8,128)(2,1)}), bf16[3584,896]{1,0:T(8,128)(2,1)}) %all-gather.5.cloned.1.call-update) | async-done | bytes 6422544 | tf_op jit(solution)/shard_map/all_gather | solution.py:88
  268.6 6.7 multiply_reduce_fusion
  275.3 8.6 psum.21
  284.3 247.6 %psum.23 = f32[896]{0:T(1024)S(1)} all-reduce(f32[896]{0:T(1024)S(1)} %fusion.29), channel_id=1, replica_groups=mesh['frames'=64,'mp'=4,'dp'=2] {'frames','dp'}, use_global_device_ids=true, to_apply=%region_9.10 | all-reduce | flops 896 | bytes 7168 | tf_op jit(solution)/shard_map/psum | solution.py:104
  532.0 0.8 multiply_convert_fusion
  532.8 1.2 multiply_multiply_fusion.1
  534.0 649.4 %psum.22 = f32[1]{0:T(128)} all-reduce(f32[1]{0:T(128)} %bitcast.11), channel_id=1, replica_groups=mesh['frames'=64,'mp'=4,'dp'=2] {'frames','mp'}, use_global_device_ids=true, to_apply=%region_8.9 | all-reduce | flops 1 | bytes 8 | tf_op jit(solution)/shard_map/psum | solution.py:99
  (53 shorter events, 6.5 us)
Async XLA Ops:
  7.2 2.0 copy-start
  7.2 98.6 %all-gather.3.cloned.1.call-start = ((), (), s32[]{:S(2)}) async-start(), calls=%async_computation | async-start | bytes 3440640 | tf_op jit(solution)/shard_map/all_gather | solution.py:84
  9.2 5.1 copy-start.2
  10.4 4.6 collective-permute-start
  13.0 6.5 collective-permute-start.1
  45.7 222.9 %all-gather.5.cloned.1.call-start = ((), (), s32[]{:S(2)}) async-start(), calls=%async_computation.1 | async-start | bytes 6522880 | tf_op jit(solution)/shard_map/all_gather | solution.py:88
  283.9 248.0 %copy-start.1 = (f32[896]{0:T(1024)S(1)}, f32[896]{0:T(1024)}, u32[]{:S(2)}) copy-start(f32[896]{0:T(1024)} %param.10) | copy-start | bytes 10756
Sparse Core Ops, SparseCore 0:
  45.8 59.8 all-gather.2
  109.0 159.5 all-gather.4
where the time goes:
time: 1190 us
  blocking collectives  906 us (76%)
  waiting for transfers between devices  227 us (19%)
  matrix products  18.3 us (2%)
  between operations  15.9 us (1%)
  local copies, waits for them, and re-layouts  13.2 us (1%)
    psum x1, blocking collectives, local(): lax.psum(local_penalty, ('frames', 'mp'))  649 us
    psum x1, blocking collectives, local(): lax.psum(feature_sums, ('frames', 'dp'))  248 us
    all_gather x1, waiting for transfers between devices, local(): lax.all_gather(out_weight, 'frames', axis=0, tiled=True)  163 us
    all_gather x1, waiting for transfers between devices, local(): gathered = lax.all_gather(attended, 'mp', axis=3, tiled=True)  59.2 us
  transfers between devices with their start and end apart: 4, of which 3 were waited for; matrix products, arithmetic and copies ran while one was open for 0% of the time, Pallas kernels for 0%

commit v1 on v0

--- a/solution.py
+++ b/solution.py
@@ -7,6 +7,11 @@
 HEAD_DIM = 128
 sigma_noise = 0.25
 epsilon = 1e-06
+
+
+def axis_by_axis(value, first, second):
+    partial = lax.psum(value, first)
+    return lax.psum(partial, second)
 
 
 def padded(cells, sides, width):
@@ -96,7 +101,7 @@
     difference = (normed[1] - normed[0]) * own_live
     feature_sums = jnp.sum(difference * difference, axis=(0, 1))
     local_penalty = jnp.sum(feature_sums * norm_gain * norm_gain).reshape(1)
-    penalty = lax.psum(local_penalty, ("frames", "mp")) / (
+    penalty = axis_by_axis(local_penalty, "frames", "mp") / (
         sigma_noise * sigma_noise * token_total * model_width
     )
     gain_grad = (

time: 1190 us -> 683 us (0.57)
  blocking collectives: 906 us -> 396 us
    psum x1 -> x2, blocking collectives: 649 us -> 140 us  [the longest x1 129 us: axis_by_axis(): partial = lax.psum(value, first)]
where the time goes in v1:
time: 683 us
  blocking collectives  396 us (58%)
  waiting for transfers between devices  227 us (33%)
  matrix products  18.3 us (3%)
  between operations  15.9 us (2%)
  local copies, waits for them, and re-layouts  13.2 us (2%)
  other arithmetic  7.59 us (1%)
    psum x1, blocking collectives, local(): lax.psum(feature_sums, ('frames', 'dp'))  248 us
    all_gather x1, waiting for transfers between devices, local(): lax.all_gather(out_weight, 'frames', axis=0, tiled=True)  163 us
    psum x1, blocking collectives, axis_by_axis(): partial = lax.psum(value, first)  129 us
    all_gather x1, waiting for transfers between devices, local(): gathered = lax.all_gather(attended, 'mp', axis=3, tiled=True)  59.2 us
  transfers between devices with their start and end apart: 4, of which 3 were waited for; matrix products, arithmetic and copies ran while one was open for 0% of the time, Pallas kernels for 0%

profile of v1, /device:TPU:2, one launch (start us, length us, event | category | flops | bytes accessed | tf_op | source)
XLA Modules:
  0.0 682.7 jit_solution(3711684249170791057)
XLA Ops:
  7.2 1.9 add_convert_fusion
  9.2 1.2 fusion.25
  10.4 2.6 collective-permute-start
  13.0 1.3 collective-permute-start.1
  15.0 4.5 collective-permute-done.1
  19.5 1.7 pad_maximum_fusion
  21.5 1.3 slice_bitcast_fusion
  22.8 22.9 %while.10 = (s32[]{:T(128)}, bf16[4,96,896]{2,1,0:T(8,128)(2,1)}, bf16[4,192,896]{2,1,0:T(8,128)(2,1)}, pred[4,192]{1,0:T(4,128)(4,1)S(1)}, bf16[4,96,896]{2,1,0...) while((s32[]{:T(128)}, bf16[4,96,896]{2,1,0:T(8,128)(2,1)}, bf16[4,192,896]{2,1,0:T(8,128)(2,1)}, ...), condition=%wide.region_3.4_spmd, body=%wide.region_0.3_spmd.sunk | while | flops 67049856 | bytes 5857369 | solution.py:64
  22.8 1.0 constant_dynamic-slice_fusion.5
  24.5 1.5 fusion.45
  26.4 1.4 fusion.46
  27.8 0.7 bitcast_dynamic-update-slice_fusion.2
  28.5 1.0 constant_dynamic-slice_fusion.5
  30.2 1.5 fusion.45
  32.1 1.4 fusion.46
  34.2 1.0 constant_dynamic-slice_fusion.5
  36.0 1.5 fusion.45
  37.9 1.4 fusion.46
  40.0 1.0 constant_dynamic-slice_fusion.5
  41.7 1.5 fusion.45
  43.6 1.4 fusion.46
  45.0 0.7 bitcast_dynamic-update-slice_fusion.2
  45.8 0.7 all-gather.5.cloned.1.call-update
  46.5 59.2 %all-gather.3.cloned.1.call-done = bf16[2,2,96,3584]{3,2,1,0:T(8,128)(2,1)} async-done(((bf16[2,2,96,896]{3,2,1,0:T(8,128)(2,1)}), bf16[2,2,96,3584]{3,2,1,0:T(8,128)(2,1)}) %all-gather.3.cloned.1.call-update) | async-done | bytes 2752528 | tf_op jit(solution)/shard_map/all_gather | solution.py:89
  105.8 162.8 %all-gather.5.cloned.1.call-done = bf16[3584,896]{1,0:T(8,128)(2,1)} async-done(((bf16[56,896]{1,0:T(8,128)(2,1)}), bf16[3584,896]{1,0:T(8,128)(2,1)}) %all-gather.5.cloned.1.call-update) | async-done | bytes 6422544 | tf_op jit(solution)/shard_map/all_gather | solution.py:93
  268.6 6.7 multiply_reduce_fusion
  275.3 8.6 %psum.28 = f32[2,2,96]{2,1,0:T(2,128)S(1)} all-reduce(f32[2,2,96]{2,1,0:T(2,128)S(1)} %get-tuple-element.58), channel_id=1, replica_groups=mesh['frames'=64,'mp'=4,'dp'=2] {'mp'}, use_global_device_ids=true, to_apply=%region_5.6 | all-reduce | flops 384 | bytes 3072 | tf_op jit(solution)/shard_map/psum | solution.py:97
  284.3 247.6 %psum.31 = f32[896]{0:T(1024)S(1)} all-reduce(f32[896]{0:T(1024)S(1)} %fusion.29), channel_id=1, replica_groups=mesh['frames'=64,'mp'=4,'dp'=2] {'frames','dp'}, use_global_device_ids=true, to_apply=%region_10.11 | all-reduce | flops 896 | bytes 7168 | tf_op jit(solution)/shard_map/psum | solution.py:109
  532.0 1.2 multiply_multiply_fusion.1
  533.2 129.4 %psum.29 = f32[1]{0:T(128)} all-reduce(f32[1]{0:T(128)} %bitcast.11), channel_id=1, replica_groups=mesh['frames'=64,'mp'=4,'dp'=2] {'frames'}, use_global_device_ids=true, to_apply=%region_8.9 | all-reduce | flops 1 | bytes 8 | tf_op jit(solution)/shard_map/psum | solution.py:13
  662.5 0.8 multiply_convert_fusion
  663.4 10.7 %psum.30 = f32[1]{0:T(128)} all-reduce(f32[1]{0:T(128)} %psum.29), channel_id=1, replica_groups=mesh['frames'=64,'mp'=4,'dp'=2] {'mp'}, use_global_device_ids=true, to_apply=%region_9.10 | all-reduce | flops 1 | bytes 8 | tf_op jit(solution)/shard_map/psum | solution.py:14
  (54 shorter events, 7.2 us)
Async XLA Ops:
  7.2 2.0 copy-start
  7.2 98.6 %all-gather.3.cloned.1.call-start = ((), (), s32[]{:S(2)}) async-start(), calls=%async_computation | async-start | bytes 3440640 | tf_op jit(solution)/shard_map/all_gather | solution.py:89
  9.2 5.1 copy-start.2
  10.4 4.6 collective-permute-start
  13.0 6.5 collective-permute-start.1
  45.7 222.9 %all-gather.5.cloned.1.call-start = ((), (), s32[]{:S(2)}) async-start(), calls=%async_computation.1 | async-start | bytes 6522880 | tf_op jit(solution)/shard_map/all_gather | solution.py:93
  283.9 248.0 %copy-start.1 = (f32[896]{0:T(1024)S(1)}, f32[896]{0:T(1024)}, u32[]{:S(2)}) copy-start(f32[896]{0:T(1024)} %param.10) | copy-start | bytes 10756
Sparse Core Ops, SparseCore 0:
  45.8 59.8 all-gather.2
  109.0 159.5 all-gather.4
